TPU v7x, 256 devices: a whole 4x4x8 slice. The times are simulated.
256 devices in a mesh: section: 16 (over z_hi, y), dp: 16 (over x, z_lo, core).
Axes of the slice: x: 4, y: 4, z: 8 (z_hi: 4, z_lo: 2; z = z_hi * 2 + z_lo), core: 2. Of those that a mesh axis runs over, the one named last changes fastest.
Arguments:
- acts: bfloat16 [16, 4, 512, 4096], P('section', None, 'dp'), may hold values from -6 to 6
- out_grad: bfloat16 [4, 512, 4096], P(None, 'dp'), may hold values from -6 to 6
- w_in: bfloat16 [16, 4096, 1152], P('section', 'dp'), may hold values from -0.09375 to 0.09375
- w_out: bfloat16 [16, 4096, 384], P('section', 'dp'), may hold values from -0.09375 to 0.09375
- decay_rate: float32 [16, 3], P('section'), may hold values from 0.004 to 0.04
- cycle_order: int32 [16], replicated, may hold values from 0 to 15, each once
Outputs:
- in_grad: bfloat16 [16, 4, 512, 4096], P('section', None, 'dp')
- grad_in: float32 [16, 4096, 1152], P('section', 'dp')
- grad_out: float32 [16, 4096, 384], P('section', 'dp')
Inputs may be any that keep to these rules, and one draw needn't show every extreme that they name: `cycle_order`: a permutation of the 16 replicas.
All inputs are finite; a program needn't handle non-finite values.
Results may differ from a plain program's by a relative error of at most 0.038.
Values may be sent and summed in bfloat16 or wider, within the bound.
A program may use at most 192 MiB of HBM per device.

v0:
```python
import jax
import jax.numpy as jnp
from jax import lax
from jax.sharding import PartitionSpec as P


def shifted(value, axis, steps):
    count = lax.axis_size(axis)
    initial, last = (max(0, -steps), min(count, count - steps))
    return lax.ppermute(value, axis, [(source, source + steps) for source in range(initial, last)])


def decay_table(rates, length):
    spots = jnp.arange(length).astype(jnp.float32)
    offset = spots[:, None] - spots[None, :]
    decayed = jnp.exp(-rates[:, None, None] * jnp.maximum(offset, 0.0)[None])
    return jnp.where(offset[None] >= 0.0, decayed, 0.0)


def contract_rows(left, right):
    return lax.dot_general(
        left, right, (((0,), (0,)), ((), ())), preferred_element_type=jnp.float32
    )


def contract_cols(left, right):
    return lax.dot_general(
        left, right, (((1,), (1,)), ((), ())), preferred_element_type=jnp.float32
    )


def retention_back(inputs, grad_y, weight_in, weight_out, table):
    length = inputs.shape[0]
    cols = weight_out.shape[1]
    heads = table.shape[0]
    head_size = cols // heads
    qkv = jnp.dot(inputs, weight_in, preferred_element_type=jnp.float32).astype(jnp.bfloat16)
    query = qkv[:, :cols].reshape(length, heads, head_size)
    keys = qkv[:, cols : 2 * cols].reshape(length, heads, head_size)
    values = qkv[:, 2 * cols :].reshape(length, heads, head_size)
    scores = (
        jnp.einsum("the,jhe->htj", query, keys, preferred_element_type=jnp.float32)
        * table
        / head_size
    ).astype(jnp.bfloat16)
    mixed = jnp.einsum("htj,jhe->the", scores, values, preferred_element_type=jnp.float32)
    mixed = mixed.reshape(length, cols).astype(jnp.bfloat16)
    d_mixed = jnp.dot(grad_y, weight_out, preferred_element_type=jnp.float32).astype(jnp.bfloat16)
    d_heads = d_mixed.reshape(length, heads, head_size)
    d_scores = (
        jnp.einsum("the,jhe->htj", d_heads, values, preferred_element_type=jnp.float32)
        * table
        / head_size
    ).astype(jnp.bfloat16)
    d_query = jnp.einsum("htj,jhe->the", d_scores, keys, preferred_element_type=jnp.float32)
    d_keys = jnp.einsum("htj,the->jhe", d_scores, query, preferred_element_type=jnp.float32)
    d_values = jnp.einsum("htj,the->jhe", scores, d_heads, preferred_element_type=jnp.float32)
    d_all = jnp.concatenate(
        [
            d_query.reshape(length, cols),
            d_keys.reshape(length, cols),
            d_values.reshape(length, cols),
        ],
        axis=1,
    ).astype(jnp.bfloat16)
    d_input = (grad_y.astype(jnp.float32) + contract_cols(d_all, weight_in)).astype(jnp.bfloat16)
    return (d_input, d_all, mixed)


def store(buffer, value, which, active):
    older = lax.dynamic_index_in_dim(buffer, which, 0, keepdims=False)
    return lax.dynamic_update_index_in_dim(buffer, jnp.where(active, value, older), which, 0)


def pass_back(d_input):
    return shifted(d_input, "section", -1)


def shards(acts, out_grad, w_in, w_out, decay_rate, cycle_order):
    sections = lax.axis_size("section")
    replicas = lax.axis_size("dp")
    place = lax.axis_index("section")
    replica = lax.axis_index("dp")
    full_in, full_out = (
        lax.all_gather(w_in[0], "dp", axis=0, tiled=True),
        lax.all_gather(w_out[0], "dp", axis=0, tiled=True),
    )
    micro = acts.shape[1]
    length = acts.shape[2]
    width = acts.shape[3]
    cols = full_out.shape[1]
    table = decay_table(decay_rate[0], length)
    saved = acts[0]
    live = jnp.where(replica == cycle_order[replicas - 1], 0.0, 1.0).astype(jnp.float32)
    last_section = sections - 1
    total_steps = micro + sections - 1

    def select(step):
        which = step - (last_section - place)
        active = jnp.logical_and(which >= 0, which < micro)
        return (jnp.clip(which, 0, micro - 1), active)

    def section_input(incoming, which):
        start_grad = lax.dynamic_index_in_dim(out_grad, which, 0, keepdims=False)
        return jnp.where(place == last_section, start_grad, incoming)

    def blank():
        return (
            jnp.zeros((length, width), jnp.bfloat16),
            jnp.zeros((length, 3 * cols), jnp.bfloat16),
            jnp.zeros((length, cols), jnp.bfloat16),
        )

    incoming0 = jnp.zeros((length, width), jnp.bfloat16)
    in_grads0 = jnp.zeros((micro, length, width), jnp.bfloat16)

    def advance(step, carry):
        incoming, in_grads, d_alls, mixes, grad_ys = carry
        which, active = select(step)
        grad_y = section_input(incoming, which)
        inputs = lax.dynamic_index_in_dim(saved, which, 0, keepdims=False)
        d_input, d_all, mixed = lax.cond(
            active, lambda: retention_back(inputs, grad_y, full_in, full_out, table), blank
        )
        in_grads = store(in_grads, d_input, which, active)
        d_alls = store(d_alls, d_all, which, active)
        mixes = store(mixes, mixed, which, active)
        grad_ys = store(grad_ys, grad_y, which, active)
        incoming = pass_back(d_input)
        return (incoming, in_grads, d_alls, mixes, grad_ys)

    start = (
        incoming0,
        in_grads0,
        jnp.zeros((micro, length, 3 * cols), jnp.bfloat16),
        jnp.zeros((micro, length, cols), jnp.bfloat16),
        jnp.zeros((micro, length, width), jnp.bfloat16),
    )
    _, in_grads, d_alls, mixes, grad_ys = lax.fori_loop(0, total_steps, advance, start)
    flat_inputs = saved.reshape(micro * length, width)
    flat_grads = grad_ys.reshape(micro * length, width)
    flat_dall = d_alls.reshape(micro * length, 3 * cols)
    flat_mixed = mixes.reshape(micro * length, cols)
    left_part = contract_rows(flat_inputs, flat_dall)
    right_part = contract_rows(flat_grads, flat_mixed)
    summed = lax.psum_scatter(
        (jnp.concatenate([left_part, right_part], axis=1) * live).astype(jnp.bfloat16),
        "dp",
        scatter_dimension=0,
        tiled=True,
    ).astype(jnp.float32)
    scale = 1.0 / (replicas - 1.0)
    grad_in = (summed[:, : 3 * cols] * scale)[None]
    grad_out = (summed[:, 3 * cols :] * scale)[None]
    return (in_grads[None], grad_in, grad_out)


def solution(mesh):
    placed = (
        P("section", None, "dp", None),
        P(None, "dp", None),
        P("section", "dp", None),
        P("section", "dp", None),
        P("section", None),
        P(),
    )
    return jax.shard_map(
        shards,
        mesh=mesh,
        in_specs=placed,
        out_specs=(
            P("section", None, "dp", None),
            P("section", "dp", None),
            P("section", "dp", None),
        ),
        check_vma=False,
    )
```

profile of v0, /device:TPU:8, one launch (start us, length us, event | category | flops | bytes accessed | tf_op | source)
XLA Modules:
  0.0 765.3 jit_solution(17528883123188055466)
XLA Ops:
  11.4 39.7 %all-gather.7.cloned.1.call-done = bf16[1,4096,384]{2,1,0:T(8,128)(2,1)} async-done(((bf16[1,256,384]{2,1,0:T(8,128)(2,1)}), bf16[1,4096,384]{2,1,0:T(8,128)(2,1)}) %all-gather.7.cloned.1.call-update) | async-done | bytes 3145744 | tf_op jit(solution)/shard_map/all_gather | solution.py:86
  51.1 61.7 %all-gather.5.cloned.1.call-done = bf16[1,4096,1152]{2,1,0:T(8,128)(2,1)} async-done(((bf16[1,256,1152]{2,1,0:T(8,128)(2,1)}), bf16[1,4096,1152]{2,1,0:T(8,128)(2,1)}) %all-gather.5.cloned.1.call-update) | async-done | bytes 9437200 | tf_op jit(solution)/shard_map/all_gather | solution.py:85
  113.1 490.0 %while.24 = (s32[]{:T(128)}, bf16[32,4096]{1,0:T(8,128)(2,1)S(1)}, bf16[4,32,4096]{2,1,0:T(8,128)(2,1)S(1)}, bf16[4,32,1152]{2,1,0:T(8,128)(2,1)S(1)}, bf16[4,32...) while((s32[]{:T(128)}, bf16[32,4096]{1,0:T(8,128)(2,1)S(1)}, ...), condition=%wide.region_3.4_spmd.clone, body=%wide.region_0.3_spmd.clone.sunk | while | flops 710326272 | bytes 56925164 | solution.py:139
  117.6 7.7 %collective-permute-done = bf16[32,4096]{1,0:T(8,128)(2,1)S(1)} collective-permute-done((bf16[32,4096]{1,0:T(8,128)(2,1)S(1)}, bf16[32,4096]{1,0:T(8,128)(2,1)S(1)}, u32[]{:S(2)}, u32[]{:S(2)}) %collective-permute-start) | collective-permute-done | bytes 262176 | tf_op jit(solution)/shard_map/while/body/eval_jaxpr/ppermute | solution.py:10
  129.7 6.9 collective-permute-done
  141.0 14.1 %collective-permute-done = bf16[32,4096]{1,0:T(8,128)(2,1)S(1)} collective-permute-done((bf16[32,4096]{1,0:T(8,128)(2,1)S(1)}, bf16[32,4096]{1,0:T(8,128)(2,1)S(1)}, u32[]{:S(2)}, u32[]{:S(2)}) %collective-permute-start) | collective-permute-done | bytes 262176 | tf_op jit(solution)/shard_map/while/body/eval_jaxpr/ppermute | solution.py:10
  159.1 13.8 %collective-permute-done = bf16[32,4096]{1,0:T(8,128)(2,1)S(1)} collective-permute-done((bf16[32,4096]{1,0:T(8,128)(2,1)S(1)}, bf16[32,4096]{1,0:T(8,128)(2,1)S(1)}, u32[]{:S(2)}, u32[]{:S(2)}) %collective-permute-start) | collective-permute-done | bytes 262176 | tf_op jit(solution)/shard_map/while/body/eval_jaxpr/ppermute | solution.py:10
  176.8 9.2 %collective-permute-done = bf16[32,4096]{1,0:T(8,128)(2,1)S(1)} collective-permute-done((bf16[32,4096]{1,0:T(8,128)(2,1)S(1)}, bf16[32,4096]{1,0:T(8,128)(2,1)S(1)}, u32[]{:S(2)}, u32[]{:S(2)}) %collective-permute-start) | collective-permute-done | bytes 262176 | tf_op jit(solution)/shard_map/while/body/eval_jaxpr/ppermute | solution.py:10
  189.9 8.6 %collective-permute-done = bf16[32,4096]{1,0:T(8,128)(2,1)S(1)} collective-permute-done((bf16[32,4096]{1,0:T(8,128)(2,1)S(1)}, bf16[32,4096]{1,0:T(8,128)(2,1)S(1)}, u32[]{:S(2)}, u32[]{:S(2)}) %collective-permute-start) | collective-permute-done | bytes 262176 | tf_op jit(solution)/shard_map/while/body/eval_jaxpr/ppermute | solution.py:10
  202.4 8.8 %collective-permute-done = bf16[32,4096]{1,0:T(8,128)(2,1)S(1)} collective-permute-done((bf16[32,4096]{1,0:T(8,128)(2,1)S(1)}, bf16[32,4096]{1,0:T(8,128)(2,1)S(1)}, u32[]{:S(2)}, u32[]{:S(2)}) %collective-permute-start) | collective-permute-done | bytes 262176 | tf_op jit(solution)/shard_map/while/body/eval_jaxpr/ppermute | solution.py:10
  215.2 9.2 %collective-permute-done = bf16[32,4096]{1,0:T(8,128)(2,1)S(1)} collective-permute-done((bf16[32,4096]{1,0:T(8,128)(2,1)S(1)}, bf16[32,4096]{1,0:T(8,128)(2,1)S(1)}, u32[]{:S(2)}, u32[]{:S(2)}) %collective-permute-start) | collective-permute-done | bytes 262176 | tf_op jit(solution)/shard_map/while/body/eval_jaxpr/ppermute | solution.py:10
  228.3 12.6 %collective-permute-done = bf16[32,4096]{1,0:T(8,128)(2,1)S(1)} collective-permute-done((bf16[32,4096]{1,0:T(8,128)(2,1)S(1)}, bf16[32,4096]{1,0:T(8,128)(2,1)S(1)}, u32[]{:S(2)}, u32[]{:S(2)}) %collective-permute-start) | collective-permute-done | bytes 262176 | tf_op jit(solution)/shard_map/while/body/eval_jaxpr/ppermute | solution.py:10
  244.9 13.2 %collective-permute-done = bf16[32,4096]{1,0:T(8,128)(2,1)S(1)} collective-permute-done((bf16[32,4096]{1,0:T(8,128)(2,1)S(1)}, bf16[32,4096]{1,0:T(8,128)(2,1)S(1)}, u32[]{:S(2)}, u32[]{:S(2)}) %collective-permute-start) | collective-permute-done | bytes 262176 | tf_op jit(solution)/shard_map/while/body/eval_jaxpr/ppermute | solution.py:10
  262.0 15.0 %collective-permute-done = bf16[32,4096]{1,0:T(8,128)(2,1)S(1)} collective-permute-done((bf16[32,4096]{1,0:T(8,128)(2,1)S(1)}, bf16[32,4096]{1,0:T(8,128)(2,1)S(1)}, u32[]{:S(2)}, u32[]{:S(2)}) %collective-permute-start) | collective-permute-done | bytes 262176 | tf_op jit(solution)/shard_map/while/body/eval_jaxpr/ppermute | solution.py:10
  281.0 11.1 %collective-permute-done = bf16[32,4096]{1,0:T(8,128)(2,1)S(1)} collective-permute-done((bf16[32,4096]{1,0:T(8,128)(2,1)S(1)}, bf16[32,4096]{1,0:T(8,128)(2,1)S(1)}, u32[]{:S(2)}, u32[]{:S(2)}) %collective-permute-start) | collective-permute-done | bytes 262176 | tf_op jit(solution)/shard_map/while/body/eval_jaxpr/ppermute | solution.py:10
  296.0 8.9 %collective-permute-done = bf16[32,4096]{1,0:T(8,128)(2,1)S(1)} collective-permute-done((bf16[32,4096]{1,0:T(8,128)(2,1)S(1)}, bf16[32,4096]{1,0:T(8,128)(2,1)S(1)}, u32[]{:S(2)}, u32[]{:S(2)}) %collective-permute-start) | collective-permute-done | bytes 262176 | tf_op jit(solution)/shard_map/while/body/eval_jaxpr/ppermute | solution.py:10
  308.8 149.8 %collective-permute-done = bf16[32,4096]{1,0:T(8,128)(2,1)S(1)} collective-permute-done((bf16[32,4096]{1,0:T(8,128)(2,1)S(1)}, bf16[32,4096]{1,0:T(8,128)(2,1)S(1)}, u32[]{:S(2)}, u32[]{:S(2)}) %collective-permute-start) | collective-permute-done | bytes 262176 | tf_op jit(solution)/shard_map/while/body/eval_jaxpr/ppermute | solution.py:10
  459.7 14.7 %conditional.3 = (bf16[32,4096]{1,0:T(8,128)(2,1)S(1)}, bf16[32,1152]{1,0:T(8,128)(2,1)}, bf16[32,384]{1,0:T(8,128)(2,1)S(1)}) conditional(s32[]{:T(128)} %convert_element_type.90, () %tuple.68, (bf16[32,4096]{1,0:T(8,128)(2,1)S(1)}, bf16[4,32,4096]{2,1,0:T(8,128)(2,1)}, s32[]{:T(128)}, bf16[4096,1152]{1,0:T(8,128)(2,1)}, ...), branch_computations={%region_1.1_spmd, %region_2.2_spmd.clone} | conditional | flops 709883904 | bytes 52238968 | solution.py:122
  462.4 5.5 convolution_convert_fusion
  477.5 9.5 %collective-permute-done = bf16[32,4096]{1,0:T(8,128)(2,1)S(1)} collective-permute-done((bf16[32,4096]{1,0:T(8,128)(2,1)S(1)}, bf16[32,4096]{1,0:T(8,128)(2,1)S(1)}, u32[]{:S(2)}, u32[]{:S(2)}) %collective-permute-start) | collective-permute-done | bytes 262176 | tf_op jit(solution)/shard_map/while/body/eval_jaxpr/ppermute | solution.py:10
  488.0 14.7 %conditional.3 = (bf16[32,4096]{1,0:T(8,128)(2,1)S(1)}, bf16[32,1152]{1,0:T(8,128)(2,1)}, bf16[32,384]{1,0:T(8,128)(2,1)S(1)}) conditional(s32[]{:T(128)} %convert_element_type.90, () %tuple.68, (bf16[32,4096]{1,0:T(8,128)(2,1)S(1)}, bf16[4,32,4096]{2,1,0:T(8,128)(2,1)}, s32[]{:T(128)}, bf16[4096,1152]{1,0:T(8,128)(2,1)}, ...), branch_computations={%region_1.1_spmd, %region_2.2_spmd.clone} | conditional | flops 709883904 | bytes 52238968 | solution.py:122
  490.7 5.5 convolution_convert_fusion
  505.8 17.3 %collective-permute-done = bf16[32,4096]{1,0:T(8,128)(2,1)S(1)} collective-permute-done((bf16[32,4096]{1,0:T(8,128)(2,1)S(1)}, bf16[32,4096]{1,0:T(8,128)(2,1)S(1)}, u32[]{:S(2)}, u32[]{:S(2)}) %collective-permute-start) | collective-permute-done | bytes 262176 | tf_op jit(solution)/shard_map/while/body/eval_jaxpr/ppermute | solution.py:10
  524.2 14.7 %conditional.3 = (bf16[32,4096]{1,0:T(8,128)(2,1)S(1)}, bf16[32,1152]{1,0:T(8,128)(2,1)}, bf16[32,384]{1,0:T(8,128)(2,1)S(1)}) conditional(s32[]{:T(128)} %convert_element_type.90, () %tuple.68, (bf16[32,4096]{1,0:T(8,128)(2,1)S(1)}, bf16[4,32,4096]{2,1,0:T(8,128)(2,1)}, s32[]{:T(128)}, bf16[4096,1152]{1,0:T(8,128)(2,1)}, ...), branch_computations={%region_1.1_spmd, %region_2.2_spmd.clone} | conditional | flops 709883904 | bytes 52238968 | solution.py:122
  526.8 5.5 convolution_convert_fusion
  542.0 15.3 %collective-permute-done = bf16[32,4096]{1,0:T(8,128)(2,1)S(1)} collective-permute-done((bf16[32,4096]{1,0:T(8,128)(2,1)S(1)}, bf16[32,4096]{1,0:T(8,128)(2,1)S(1)}, u32[]{:S(2)}, u32[]{:S(2)}) %collective-permute-start) | collective-permute-done | bytes 262176 | tf_op jit(solution)/shard_map/while/body/eval_jaxpr/ppermute | solution.py:10
  558.4 14.7 %conditional.3 = (bf16[32,4096]{1,0:T(8,128)(2,1)S(1)}, bf16[32,1152]{1,0:T(8,128)(2,1)}, bf16[32,384]{1,0:T(8,128)(2,1)S(1)}) conditional(s32[]{:T(128)} %convert_element_type.90, () %tuple.68, (bf16[32,4096]{1,0:T(8,128)(2,1)S(1)}, bf16[4,32,4096]{2,1,0:T(8,128)(2,1)}, s32[]{:T(128)}, bf16[4096,1152]{1,0:T(8,128)(2,1)}, ...), branch_computations={%region_1.1_spmd, %region_2.2_spmd.clone} | conditional | flops 709883904 | bytes 52238968 | solution.py:122
  561.0 5.5 convolution_convert_fusion
  576.1 5.2 collective-permute-done
  583.2 16.0 %collective-permute-start = (bf16[32,4096]{1,0:T(8,128)(2,1)S(1)}, bf16[32,4096]{1,0:T(8,128)(2,1)S(1)}, u32[]{:S(2)}, u32[]{:S(2)}) collective-permute-start(bf16[32,4096]{1,0:T(8,128)(2,1)S(1)} %get-tuple-element.528), channel_id=1, source_target_pairs={{16,0},{32,16},{48,32},{64,48},{80,64},{96,80},{112,96},{128,112},... | collective-permute-start | bytes 786440 | tf_op jit(solution)/shard_map/while/body/eval_jaxpr/ppermute | solution.py:10
  607.9 9.0 %fusion.32 = bf16[4096,1536]{0,1:T(8,128)(2,1)} fusion(f32[4096,384]{0,1:T(8,128)S(1)} %convolution_bitcast_fusion.1, f32[4096,1152]{0,1:T(8,128)S(1)} %convolution_bitcast_fusion, f32[]{:T(128)S(6)} %select_n.115), kind=kLoop, calls=%fused_computation.62 | loop fusion | flops 18874368 | bytes 37748740 | tf_op jit(solution)/shard_map/convert_element_type | solution.py:147
  617.0 138.1 %reduce-scatter.2.cloned.1.call-done = bf16[256,1536]{0,1:T(8,128)(2,1)} async-done(((bf16[4096,1536]{0,1:T(8,128)(2,1)}), bf16[256,1536]{0,1:T(8,128)(2,1)}) %reduce-scatter.2.cloned.1.call-update) | async-done | bytes 786448 | tf_op jit(solution)/shard_map/reduce_scatter | solution.py:146
  (336 shorter events, 136.6 us)
Async XLA Ops:
  7.2 43.9 %all-gather.7.cloned.1.call-start = ((), (), s32[]{:S(2)}) async-start(), calls=%async_computation.3 | async-start | bytes 3342336 | tf_op jit(solution)/shard_map/all_gather | solution.py:86
  7.9 104.9 %all-gather.5.cloned.1.call-start = ((), (), s32[]{:S(2)}) async-start(), calls=%async_computation.2 | async-start | bytes 10027008 | tf_op jit(solution)/shard_map/all_gather | solution.py:85
  8.6 746.4 %reduce-scatter.2.cloned.1.call-start = ((), (), s32[]{:S(2)}) async-start(), calls=%async_computation.1 | async-start | bytes 13369344 | tf_op jit(solution)/shard_map/reduce_scatter | solution.py:146
  114.9 10.4 %collective-permute-start = (bf16[32,4096]{1,0:T(8,128)(2,1)S(1)}, bf16[32,4096]{1,0:T(8,128)(2,1)S(1)}, u32[]{:S(2)}, u32[]{:S(2)}) collective-permute-start(bf16[32,4096]{1,0:T(8,128)(2,1)S(1)} %get-tuple-element.528), channel_id=1, source_target_pairs={{16,0},{32,16},{48,32},{64,48},{80,64},{96,80},{112,96},{128,112},... | collective-permute-start | bytes 786440 | tf_op jit(solution)/shard_map/while/body/eval_jaxpr/ppermute | solution.py:10
  127.0 9.5 %collective-permute-start = (bf16[32,4096]{1,0:T(8,128)(2,1)S(1)}, bf16[32,4096]{1,0:T(8,128)(2,1)S(1)}, u32[]{:S(2)}, u32[]{:S(2)}) collective-permute-start(bf16[32,4096]{1,0:T(8,128)(2,1)S(1)} %get-tuple-element.528), channel_id=1, source_target_pairs={{16,0},{32,16},{48,32},{64,48},{80,64},{96,80},{112,96},{128,112},... | collective-permute-start | bytes 786440 | tf_op jit(solution)/shard_map/while/body/eval_jaxpr/ppermute | solution.py:10
  138.4 16.8 %collective-permute-start = (bf16[32,4096]{1,0:T(8,128)(2,1)S(1)}, bf16[32,4096]{1,0:T(8,128)(2,1)S(1)}, u32[]{:S(2)}, u32[]{:S(2)}) collective-permute-start(bf16[32,4096]{1,0:T(8,128)(2,1)S(1)} %get-tuple-element.528), channel_id=1, source_target_pairs={{16,0},{32,16},{48,32},{64,48},{80,64},{96,80},{112,96},{128,112},... | collective-permute-start | bytes 786440 | tf_op jit(solution)/shard_map/while/body/eval_jaxpr/ppermute | solution.py:10
  156.9 15.9 %collective-permute-start = (bf16[32,4096]{1,0:T(8,128)(2,1)S(1)}, bf16[32,4096]{1,0:T(8,128)(2,1)S(1)}, u32[]{:S(2)}, u32[]{:S(2)}) collective-permute-start(bf16[32,4096]{1,0:T(8,128)(2,1)S(1)} %get-tuple-element.528), channel_id=1, source_target_pairs={{16,0},{32,16},{48,32},{64,48},{80,64},{96,80},{112,96},{128,112},... | collective-permute-start | bytes 786440 | tf_op jit(solution)/shard_map/while/body/eval_jaxpr/ppermute | solution.py:10
  174.7 11.3 %collective-permute-start = (bf16[32,4096]{1,0:T(8,128)(2,1)S(1)}, bf16[32,4096]{1,0:T(8,128)(2,1)S(1)}, u32[]{:S(2)}, u32[]{:S(2)}) collective-permute-start(bf16[32,4096]{1,0:T(8,128)(2,1)S(1)} %get-tuple-element.528), channel_id=1, source_target_pairs={{16,0},{32,16},{48,32},{64,48},{80,64},{96,80},{112,96},{128,112},... | collective-permute-start | bytes 786440 | tf_op jit(solution)/shard_map/while/body/eval_jaxpr/ppermute | solution.py:10
  187.8 10.7 %collective-permute-start = (bf16[32,4096]{1,0:T(8,128)(2,1)S(1)}, bf16[32,4096]{1,0:T(8,128)(2,1)S(1)}, u32[]{:S(2)}, u32[]{:S(2)}) collective-permute-start(bf16[32,4096]{1,0:T(8,128)(2,1)S(1)} %get-tuple-element.528), channel_id=1, source_target_pairs={{16,0},{32,16},{48,32},{64,48},{80,64},{96,80},{112,96},{128,112},... | collective-permute-start | bytes 786440 | tf_op jit(solution)/shard_map/while/body/eval_jaxpr/ppermute | solution.py:10
  200.3 11.0 %collective-permute-start = (bf16[32,4096]{1,0:T(8,128)(2,1)S(1)}, bf16[32,4096]{1,0:T(8,128)(2,1)S(1)}, u32[]{:S(2)}, u32[]{:S(2)}) collective-permute-start(bf16[32,4096]{1,0:T(8,128)(2,1)S(1)} %get-tuple-element.528), channel_id=1, source_target_pairs={{16,0},{32,16},{48,32},{64,48},{80,64},{96,80},{112,96},{128,112},... | collective-permute-start | bytes 786440 | tf_op jit(solution)/shard_map/while/body/eval_jaxpr/ppermute | solution.py:10
  213.1 11.3 %collective-permute-start = (bf16[32,4096]{1,0:T(8,128)(2,1)S(1)}, bf16[32,4096]{1,0:T(8,128)(2,1)S(1)}, u32[]{:S(2)}, u32[]{:S(2)}) collective-permute-start(bf16[32,4096]{1,0:T(8,128)(2,1)S(1)} %get-tuple-element.528), channel_id=1, source_target_pairs={{16,0},{32,16},{48,32},{64,48},{80,64},{96,80},{112,96},{128,112},... | collective-permute-start | bytes 786440 | tf_op jit(solution)/shard_map/while/body/eval_jaxpr/ppermute | solution.py:10
  226.2 14.8 %collective-permute-start = (bf16[32,4096]{1,0:T(8,128)(2,1)S(1)}, bf16[32,4096]{1,0:T(8,128)(2,1)S(1)}, u32[]{:S(2)}, u32[]{:S(2)}) collective-permute-start(bf16[32,4096]{1,0:T(8,128)(2,1)S(1)} %get-tuple-element.528), channel_id=1, source_target_pairs={{16,0},{32,16},{48,32},{64,48},{80,64},{96,80},{112,96},{128,112},... | collective-permute-start | bytes 786440 | tf_op jit(solution)/shard_map/while/body/eval_jaxpr/ppermute | solution.py:10
  242.8 15.3 %collective-permute-start = (bf16[32,4096]{1,0:T(8,128)(2,1)S(1)}, bf16[32,4096]{1,0:T(8,128)(2,1)S(1)}, u32[]{:S(2)}, u32[]{:S(2)}) collective-permute-start(bf16[32,4096]{1,0:T(8,128)(2,1)S(1)} %get-tuple-element.528), channel_id=1, source_target_pairs={{16,0},{32,16},{48,32},{64,48},{80,64},{96,80},{112,96},{128,112},... | collective-permute-start | bytes 786440 | tf_op jit(solution)/shard_map/while/body/eval_jaxpr/ppermute | solution.py:10
  259.9 17.2 %collective-permute-start = (bf16[32,4096]{1,0:T(8,128)(2,1)S(1)}, bf16[32,4096]{1,0:T(8,128)(2,1)S(1)}, u32[]{:S(2)}, u32[]{:S(2)}) collective-permute-start(bf16[32,4096]{1,0:T(8,128)(2,1)S(1)} %get-tuple-element.528), channel_id=1, source_target_pairs={{16,0},{32,16},{48,32},{64,48},{80,64},{96,80},{112,96},{128,112},... | collective-permute-start | bytes 786440 | tf_op jit(solution)/shard_map/while/body/eval_jaxpr/ppermute | solution.py:10
  278.8 13.2 %collective-permute-start = (bf16[32,4096]{1,0:T(8,128)(2,1)S(1)}, bf16[32,4096]{1,0:T(8,128)(2,1)S(1)}, u32[]{:S(2)}, u32[]{:S(2)}) collective-permute-start(bf16[32,4096]{1,0:T(8,128)(2,1)S(1)} %get-tuple-element.528), channel_id=1, source_target_pairs={{16,0},{32,16},{48,32},{64,48},{80,64},{96,80},{112,96},{128,112},... | collective-permute-start | bytes 786440 | tf_op jit(solution)/shard_map/while/body/eval_jaxpr/ppermute | solution.py:10
  293.8 11.0 %collective-permute-start = (bf16[32,4096]{1,0:T(8,128)(2,1)S(1)}, bf16[32,4096]{1,0:T(8,128)(2,1)S(1)}, u32[]{:S(2)}, u32[]{:S(2)}) collective-permute-start(bf16[32,4096]{1,0:T(8,128)(2,1)S(1)} %get-tuple-element.528), channel_id=1, source_target_pairs={{16,0},{32,16},{48,32},{64,48},{80,64},{96,80},{112,96},{128,112},... | collective-permute-start | bytes 786440 | tf_op jit(solution)/shard_map/while/body/eval_jaxpr/ppermute | solution.py:10
  306.7 152.0 %collective-permute-start = (bf16[32,4096]{1,0:T(8,128)(2,1)S(1)}, bf16[32,4096]{1,0:T(8,128)(2,1)S(1)}, u32[]{:S(2)}, u32[]{:S(2)}) collective-permute-start(bf16[32,4096]{1,0:T(8,128)(2,1)S(1)} %get-tuple-element.528), channel_id=1, source_target_pairs={{16,0},{32,16},{48,32},{64,48},{80,64},{96,80},{112,96},{128,112},... | collective-permute-start | bytes 786440 | tf_op jit(solution)/shard_map/while/body/eval_jaxpr/ppermute | solution.py:10
  459.7 10.9 %slice-start = ((s8[9437184]{0:T(1024)(128)(4,1)}), s8[4194304]{0:T(1024)(128)(4,1)S(1)}, s32[]{:S(2)}) async-start(s8[9437184]{0:T(1024)(128)(4,1)} %bitcast.131), calls=%async_computation.4 | async-start | bytes 8388608 | tf_op jit(solution)/shard_map/while/body/eval_jaxpr/cond
  462.3 8.3 %slice-start.1 = ((s8[9437184]{0:T(1024)(128)(4,1)}), s8[4194304]{0:T(1024)(128)(4,1)S(1)}, s32[]{:S(2)}) async-start(s8[9437184]{0:T(1024)(128)(4,1)} %bitcast.131), calls=%async_computation.5 | async-start | bytes 8388608 | tf_op jit(solution)/shard_map/while/body/eval_jaxpr/cond
  462.4 8.3 %slice-start.2 = ((s8[9437184]{0:T(1024)(128)(4,1)}), s8[1048576]{0:T(1024)(128)(4,1)S(1)}, s32[]{:S(2)}) async-start(s8[9437184]{0:T(1024)(128)(4,1)} %bitcast.131), calls=%async_computation.6 | async-start | bytes 2097152 | tf_op jit(solution)/shard_map/while/body/eval_jaxpr/cond
  474.5 12.5 %collective-permute-start = (bf16[32,4096]{1,0:T(8,128)(2,1)S(1)}, bf16[32,4096]{1,0:T(8,128)(2,1)S(1)}, u32[]{:S(2)}, u32[]{:S(2)}) collective-permute-start(bf16[32,4096]{1,0:T(8,128)(2,1)S(1)} %get-tuple-element.528), channel_id=1, source_target_pairs={{16,0},{32,16},{48,32},{64,48},{80,64},{96,80},{112,96},{128,112},... | collective-permute-start | bytes 786440 | tf_op jit(solution)/shard_map/while/body/eval_jaxpr/ppermute | solution.py:10
  488.1 10.9 %slice-start = ((s8[9437184]{0:T(1024)(128)(4,1)}), s8[4194304]{0:T(1024)(128)(4,1)S(1)}, s32[]{:S(2)}) async-start(s8[9437184]{0:T(1024)(128)(4,1)} %bitcast.131), calls=%async_computation.4 | async-start | bytes 8388608 | tf_op jit(solution)/shard_map/while/body/eval_jaxpr/cond
  490.7 8.3 %slice-start.1 = ((s8[9437184]{0:T(1024)(128)(4,1)}), s8[4194304]{0:T(1024)(128)(4,1)S(1)}, s32[]{:S(2)}) async-start(s8[9437184]{0:T(1024)(128)(4,1)} %bitcast.131), calls=%async_computation.5 | async-start | bytes 8388608 | tf_op jit(solution)/shard_map/while/body/eval_jaxpr/cond
  490.7 8.3 %slice-start.2 = ((s8[9437184]{0:T(1024)(128)(4,1)}), s8[1048576]{0:T(1024)(128)(4,1)S(1)}, s32[]{:S(2)}) async-start(s8[9437184]{0:T(1024)(128)(4,1)} %bitcast.131), calls=%async_computation.6 | async-start | bytes 2097152 | tf_op jit(solution)/shard_map/while/body/eval_jaxpr/cond
  502.8 20.3 %collective-permute-start = (bf16[32,4096]{1,0:T(8,128)(2,1)S(1)}, bf16[32,4096]{1,0:T(8,128)(2,1)S(1)}, u32[]{:S(2)}, u32[]{:S(2)}) collective-permute-start(bf16[32,4096]{1,0:T(8,128)(2,1)S(1)} %get-tuple-element.528), channel_id=1, source_target_pairs={{16,0},{32,16},{48,32},{64,48},{80,64},{96,80},{112,96},{128,112},... | collective-permute-start | bytes 786440 | tf_op jit(solution)/shard_map/while/body/eval_jaxpr/ppermute | solution.py:10
  524.2 10.9 %slice-start = ((s8[9437184]{0:T(1024)(128)(4,1)}), s8[4194304]{0:T(1024)(128)(4,1)S(1)}, s32[]{:S(2)}) async-start(s8[9437184]{0:T(1024)(128)(4,1)} %bitcast.131), calls=%async_computation.4 | async-start | bytes 8388608 | tf_op jit(solution)/shard_map/while/body/eval_jaxpr/cond
  526.8 8.3 %slice-start.1 = ((s8[9437184]{0:T(1024)(128)(4,1)}), s8[4194304]{0:T(1024)(128)(4,1)S(1)}, s32[]{:S(2)}) async-start(s8[9437184]{0:T(1024)(128)(4,1)} %bitcast.131), calls=%async_computation.5 | async-start | bytes 8388608 | tf_op jit(solution)/shard_map/while/body/eval_jaxpr/cond
  538.9 18.3 %collective-permute-start = (bf16[32,4096]{1,0:T(8,128)(2,1)S(1)}, bf16[32,4096]{1,0:T(8,128)(2,1)S(1)}, u32[]{:S(2)}, u32[]{:S(2)}) collective-permute-start(bf16[32,4096]{1,0:T(8,128)(2,1)S(1)} %get-tuple-element.528), channel_id=1, source_target_pairs={{16,0},{32,16},{48,32},{64,48},{80,64},{96,80},{112,96},{128,112},... | collective-permute-start | bytes 786440 | tf_op jit(solution)/shard_map/while/body/eval_jaxpr/ppermute | solution.py:10
  558.4 10.9 %slice-start = ((s8[9437184]{0:T(1024)(128)(4,1)}), s8[4194304]{0:T(1024)(128)(4,1)S(1)}, s32[]{:S(2)}) async-start(s8[9437184]{0:T(1024)(128)(4,1)} %bitcast.131), calls=%async_computation.4 | async-start | bytes 8388608 | tf_op jit(solution)/shard_map/while/body/eval_jaxpr/cond
  561.0 8.3 %slice-start.1 = ((s8[9437184]{0:T(1024)(128)(4,1)}), s8[4194304]{0:T(1024)(128)(4,1)S(1)}, s32[]{:S(2)}) async-start(s8[9437184]{0:T(1024)(128)(4,1)} %bitcast.131), calls=%async_computation.5 | async-start | bytes 8388608 | tf_op jit(solution)/shard_map/while/body/eval_jaxpr/cond
  573.1 8.3 %collective-permute-start = (bf16[32,4096]{1,0:T(8,128)(2,1)S(1)}, bf16[32,4096]{1,0:T(8,128)(2,1)S(1)}, u32[]{:S(2)}, u32[]{:S(2)}) collective-permute-start(bf16[32,4096]{1,0:T(8,128)(2,1)S(1)} %get-tuple-element.528), channel_id=1, source_target_pairs={{16,0},{32,16},{48,32},{64,48},{80,64},{96,80},{112,96},{128,112},... | collective-permute-start | bytes 786440 | tf_op jit(solution)/shard_map/while/body/eval_jaxpr/ppermute | solution.py:10
  583.2 19.8 %collective-permute-start = (bf16[32,4096]{1,0:T(8,128)(2,1)S(1)}, bf16[32,4096]{1,0:T(8,128)(2,1)S(1)}, u32[]{:S(2)}, u32[]{:S(2)}) collective-permute-start(bf16[32,4096]{1,0:T(8,128)(2,1)S(1)} %get-tuple-element.528), channel_id=1, source_target_pairs={{16,0},{32,16},{48,32},{64,48},{80,64},{96,80},{112,96},{128,112},... | collective-permute-start | bytes 786440 | tf_op jit(solution)/shard_map/while/body/eval_jaxpr/ppermute | solution.py:10
  (3 other events, 21.6 us)
Sparse Core Ops, SparseCore 0:
  9.8 41.1 all-gather.6
  52.9 59.8 all-gather.4
  617.1 137.9 reduce-scatter.1
where the time goes:
time: 767 us; the launch traced here: 765 us
  waiting for transfers between devices  581 us (76%)
  matrix products  55.9 us (7%)
  starting transfers between devices  52.2 us (7%)
  other arithmetic  37.4 us (5%)
  local copies, waits for them, and re-layouts  22.7 us (3%)
  between operations  14.5 us (2%)
    ppermute x19, waiting for transfers between devices, shifted(): lax.ppermute(value, axis, [(source, source + steps) for source in range(i...  340 us
    reduce_scatter x1, waiting for transfers between devices, shards(): lax.psum_scatter((jnp.concatenate([left_part, right_part], axis=1) * live...  138 us
    all_gather x1, waiting for transfers between devices, shards(): lax.all_gather(w_in[0], 'dp', axis=0, tiled=True)  61.7 us
    ppermute x19, starting transfers between devices, shifted(): lax.ppermute(value, axis, [(source, source + steps) for source in range(i...  52.1 us
    all_gather x1, waiting for transfers between devices, shards(): lax.all_gather(w_out[0], 'dp', axis=0, tiled=True)  39.7 us
    dynamic_update_slice x76, other arithmetic, store(): lax.dynamic_update_index_in_dim(buffer, jnp.where(active, value, older),...  26.2 us
    dot_general x4, matrix products, retention_back(): jnp.dot(inputs, weight_in, preferred_element_type=jnp.float32)  22 us
  transfers between devices with their start and end apart: 22, of which 22 were waited for; matrix products, arithmetic and copies ran while one was open for 1% of the time, Pallas kernels for 0%

commit v1 on v0

--- a/solution.py
+++ b/solution.py
@@ -82,7 +82,9 @@
     place = lax.axis_index("section")
     replica = lax.axis_index("dp")
     full_in, full_out = (
-        lax.all_gather(w_in[0], "dp", axis=0, tiled=True),
+        jnp.concatenate(
+            lax.all_to_all(jnp.stack([w_in[0]] * lax.axis_size("dp")), "dp", 0, 0), axis=0
+        ),
         lax.all_gather(w_out[0], "dp", axis=0, tiled=True),
     )
     micro = acts.shape[1]

time: 767 us -> 847 us (1.10)
  local copies, waits for them, and re-layouts: 22.7 us -> 46.9 us
  waiting for transfers between devices: 581 us -> 601 us
  starting transfers between devices: 52.2 us -> 65.5 us
  other arithmetic: 37.4 us -> 49.9 us
  matrix products: 55.9 us -> 64.5 us
    all_gather x1, waiting for transfers between devices: 39.7 us -> 124 us  [shards(): lax.all_gather(w_out[0], 'dp', axis=0, tiled=True)]
    all_gather x1 -> x0, waiting for transfers between devices: 61.7 us -> none  [shards(): lax.all_gather(w_in[0], 'dp', axis=0, tiled=True)]
    dynamic_slice x76, local copies, waits for them, and re-layouts: 1.36 us -> 19.3 us  [store(): older = lax.dynamic_index_in_dim(buffer, which, 0, keepdims=False)]
    dynamic_update_slice x76, other arithmetic: 26.2 us -> 39.4 us  [store(): lax.dynamic_update_index_in_dim(buffer, jnp.where(active, value, older),...]
    dot_general x4, matrix products: 15 us -> 26.4 us  [contract_cols(): lax.dot_general(left, right, (((1,), (1,)), ((), ())), preferred_element_...]
    another operation x48 -> x49, local copies, waits for them, and re-layouts: 10.2 us -> 17.2 us
  transfers between devices with their start and end apart: 22 -> 22, of which waited for: 22 -> 22; matrix products, arithmetic and copies ran while one was open for 1% -> 5% of each run, Pallas kernels for 0% -> 0%
where the time goes in v1:
time: 847 us; the launch traced here: 845 us
  waiting for transfers between devices  601 us (71%)
  starting transfers between devices  65.5 us (8%)
  matrix products  64.5 us (8%)
  other arithmetic  49.9 us (6%)
  local copies, waits for them, and re-layouts  46.9 us (6%)
  between operations  14.8 us (2%)
    ppermute x19, waiting for transfers between devices, shifted(): lax.ppermute(value, axis, [(source, source + steps) for source in range(i...  332 us
    reduce_scatter x1, waiting for transfers between devices, shards(): lax.psum_scatter((jnp.concatenate([left_part, right_part], axis=1) * live...  140 us
    all_gather x1, waiting for transfers between devices, shards(): lax.all_gather(w_out[0], 'dp', axis=0, tiled=True)  124 us
    ppermute x19, starting transfers between devices, shifted(): lax.ppermute(value, axis, [(source, source + steps) for source in range(i...  59.5 us
    dynamic_update_slice x76, other arithmetic, store(): lax.dynamic_update_index_in_dim(buffer, jnp.where(active, value, older),...  39.4 us
    dot_general x4, matrix products, contract_cols(): lax.dot_general(left, right, (((1,), (1,)), ((), ())), preferred_element_...  26.4 us
    dot_general x4, matrix products, retention_back(): jnp.dot(inputs, weight_in, preferred_element_type=jnp.float32)  21.1 us
    dynamic_slice x76, local copies, waits for them, and re-layouts, store(): older = lax.dynamic_index_in_dim(buffer, which, 0, keepdims=False)  19.3 us
  transfers between devices with their start and end apart: 22, of which 22 were waited for; matrix products, arithmetic and copies ran while one was open for 5% of the time, Pallas kernels for 0%

profile of v1, /device:TPU:8, one launch (start us, length us, event | category | flops | bytes accessed | tf_op | source)
XLA Modules:
  0.0 844.7 jit_solution(11814875158643103955)
XLA Ops:
  7.2 6.0 stack.3
  13.1 5.9 all-to-all-start
  21.3 123.9 %all-gather.3.cloned.1.call-done = bf16[1,4096,384]{2,1,0:T(8,128)(2,1)} async-done(((bf16[1,256,384]{2,1,0:T(8,128)(2,1)}), bf16[1,4096,384]{2,1,0:T(8,128)(2,1)}) %all-gather.3.cloned.1.call-update) | async-done | bytes 3145744 | tf_op jit(solution)/shard_map/all_gather | solution.py:88
  151.2 530.5 %while.24 = (s32[]{:T(128)}, bf16[32,4096]{1,0:T(8,128)(2,1)S(1)}, bf16[4,32,4096]{2,1,0:T(8,128)(2,1)}, bf16[4,32,1152]{2,1,0:T(8,128)(2,1)S(1)}, bf16[4,32,384...) while((s32[]{:T(128)}, bf16[32,4096]{1,0:T(8,128)(2,1)S(1)}, ...), condition=%wide.region_3.4_spmd.clone, body=%wide.region_0.3_spmd.clone.sunk | while | flops 710326272 | bytes 28613540 | solution.py:141
  181.2 10.4 %collective-permute-done = bf16[32,4096]{1,0:T(8,128)(2,1)S(1)} collective-permute-done((bf16[32,4096]{1,0:T(8,128)(2,1)S(1)}, bf16[32,4096]{1,0:T(8,128)(2,1)S(1)}, u32[]{:S(2)}, u32[]{:S(2)}) %collective-permute-start) | collective-permute-done | bytes 262176 | tf_op jit(solution)/shard_map/while/body/eval_jaxpr/ppermute | solution.py:10
  197.1 7.5 collective-permute-done
  210.2 12.3 %collective-permute-done = bf16[32,4096]{1,0:T(8,128)(2,1)S(1)} collective-permute-done((bf16[32,4096]{1,0:T(8,128)(2,1)S(1)}, bf16[32,4096]{1,0:T(8,128)(2,1)S(1)}, u32[]{:S(2)}, u32[]{:S(2)}) %collective-permute-start) | collective-permute-done | bytes 262176 | tf_op jit(solution)/shard_map/while/body/eval_jaxpr/ppermute | solution.py:10
  228.1 8.5 %collective-permute-done = bf16[32,4096]{1,0:T(8,128)(2,1)S(1)} collective-permute-done((bf16[32,4096]{1,0:T(8,128)(2,1)S(1)}, bf16[32,4096]{1,0:T(8,128)(2,1)S(1)}, u32[]{:S(2)}, u32[]{:S(2)}) %collective-permute-start) | collective-permute-done | bytes 262176 | tf_op jit(solution)/shard_map/while/body/eval_jaxpr/ppermute | solution.py:10
  242.2 6.9 collective-permute-done
  254.7 13.5 %collective-permute-done = bf16[32,4096]{1,0:T(8,128)(2,1)S(1)} collective-permute-done((bf16[32,4096]{1,0:T(8,128)(2,1)S(1)}, bf16[32,4096]{1,0:T(8,128)(2,1)S(1)}, u32[]{:S(2)}, u32[]{:S(2)}) %collective-permute-start) | collective-permute-done | bytes 262176 | tf_op jit(solution)/shard_map/while/body/eval_jaxpr/ppermute | solution.py:10
  273.8 8.6 %collective-permute-done = bf16[32,4096]{1,0:T(8,128)(2,1)S(1)} collective-permute-done((bf16[32,4096]{1,0:T(8,128)(2,1)S(1)}, bf16[32,4096]{1,0:T(8,128)(2,1)S(1)}, u32[]{:S(2)}, u32[]{:S(2)}) %collective-permute-start) | collective-permute-done | bytes 262176 | tf_op jit(solution)/shard_map/while/body/eval_jaxpr/ppermute | solution.py:10
  287.9 11.3 %collective-permute-done = bf16[32,4096]{1,0:T(8,128)(2,1)S(1)} collective-permute-done((bf16[32,4096]{1,0:T(8,128)(2,1)S(1)}, bf16[32,4096]{1,0:T(8,128)(2,1)S(1)}, u32[]{:S(2)}, u32[]{:S(2)}) %collective-permute-start) | collective-permute-done | bytes 262176 | tf_op jit(solution)/shard_map/while/body/eval_jaxpr/ppermute | solution.py:10
  304.8 8.1 collective-permute-done
  318.4 7.5 collective-permute-done
  331.5 7.5 collective-permute-done
  344.6 185.4 %collective-permute-done = bf16[32,4096]{1,0:T(8,128)(2,1)S(1)} collective-permute-done((bf16[32,4096]{1,0:T(8,128)(2,1)S(1)}, bf16[32,4096]{1,0:T(8,128)(2,1)S(1)}, u32[]{:S(2)}, u32[]{:S(2)}) %collective-permute-start) | collective-permute-done | bytes 262176 | tf_op jit(solution)/shard_map/while/body/eval_jaxpr/ppermute | solution.py:10
  531.0 17.1 %conditional.3 = (bf16[32,4096]{1,0:T(8,128)(2,1)S(1)}, bf16[32,1152]{1,0:T(8,128)(2,1)}, bf16[32,384]{1,0:T(8,128)(2,1)S(1)}) conditional(s32[]{:T(128)} %convert_element_type.90, () %tuple.68, (bf16[32,4096]{1,0:T(8,128)(2,1)S(1)}, bf16[4,32,4096]{2,1,0:T(8,128)(2,1)S(1)}, s32[]{:T(128)}, bf16[4096,1152]{1,0:T(8,128)(2,1)}, ...), branch_computations={%region_1.1_spmd, %region_2.2_spmd.clone} | conditional | flops 709883904 | bytes 23926836 | solution.py:124
  533.5 5.3 convolution_convert_fusion
  541.6 6.6 fusion.2
  552.8 8.0 collective-permute-done
  561.9 17.1 %conditional.3 = (bf16[32,4096]{1,0:T(8,128)(2,1)S(1)}, bf16[32,1152]{1,0:T(8,128)(2,1)}, bf16[32,384]{1,0:T(8,128)(2,1)S(1)}) conditional(s32[]{:T(128)} %convert_element_type.90, () %tuple.68, (bf16[32,4096]{1,0:T(8,128)(2,1)S(1)}, bf16[4,32,4096]{2,1,0:T(8,128)(2,1)S(1)}, s32[]{:T(128)}, bf16[4096,1152]{1,0:T(8,128)(2,1)}, ...), branch_computations={%region_1.1_spmd, %region_2.2_spmd.clone} | conditional | flops 709883904 | bytes 23926836 | solution.py:124
  572.5 6.6 fusion.2
  583.7 12.2 %collective-permute-done = bf16[32,4096]{1,0:T(8,128)(2,1)S(1)} collective-permute-done((bf16[32,4096]{1,0:T(8,128)(2,1)S(1)}, bf16[32,4096]{1,0:T(8,128)(2,1)S(1)}, u32[]{:S(2)}, u32[]{:S(2)}) %collective-permute-start) | collective-permute-done | bytes 262176 | tf_op jit(solution)/shard_map/while/body/eval_jaxpr/ppermute | solution.py:10
  597.0 17.1 %conditional.3 = (bf16[32,4096]{1,0:T(8,128)(2,1)S(1)}, bf16[32,1152]{1,0:T(8,128)(2,1)}, bf16[32,384]{1,0:T(8,128)(2,1)S(1)}) conditional(s32[]{:T(128)} %convert_element_type.90, () %tuple.68, (bf16[32,4096]{1,0:T(8,128)(2,1)S(1)}, bf16[4,32,4096]{2,1,0:T(8,128)(2,1)S(1)}, s32[]{:T(128)}, bf16[4096,1152]{1,0:T(8,128)(2,1)}, ...), branch_computations={%region_1.1_spmd, %region_2.2_spmd.clone} | conditional | flops 709883904 | bytes 23926836 | solution.py:124
  599.5 5.3 convolution_convert_fusion
  607.6 6.6 fusion.2
  618.8 12.4 %collective-permute-done = bf16[32,4096]{1,0:T(8,128)(2,1)S(1)} collective-permute-done((bf16[32,4096]{1,0:T(8,128)(2,1)S(1)}, bf16[32,4096]{1,0:T(8,128)(2,1)S(1)}, u32[]{:S(2)}, u32[]{:S(2)}) %collective-permute-start) | collective-permute-done | bytes 262176 | tf_op jit(solution)/shard_map/while/body/eval_jaxpr/ppermute | solution.py:10
  632.3 17.1 %conditional.3 = (bf16[32,4096]{1,0:T(8,128)(2,1)S(1)}, bf16[32,1152]{1,0:T(8,128)(2,1)}, bf16[32,384]{1,0:T(8,128)(2,1)S(1)}) conditional(s32[]{:T(128)} %convert_element_type.90, () %tuple.68, (bf16[32,4096]{1,0:T(8,128)(2,1)S(1)}, bf16[4,32,4096]{2,1,0:T(8,128)(2,1)S(1)}, s32[]{:T(128)}, bf16[4096,1152]{1,0:T(8,128)(2,1)}, ...), branch_computations={%region_1.1_spmd, %region_2.2_spmd.clone} | conditional | flops 709883904 | bytes 23926836 | solution.py:124
  642.9 6.6 fusion.2
  659.5 18.4 %collective-permute-start = (bf16[32,4096]{1,0:T(8,128)(2,1)S(1)}, bf16[32,4096]{1,0:T(8,128)(2,1)S(1)}, u32[]{:S(2)}, u32[]{:S(2)}) collective-permute-start(bf16[32,4096]{1,0:T(8,128)(2,1)S(1)} %get-tuple-element.528), channel_id=1, source_target_pairs={{16,0},{32,16},{48,32},{64,48},{80,64},{96,80},{112,96},{128,112},... | collective-permute-start | bytes 786440 | tf_op jit(solution)/shard_map/while/body/eval_jaxpr/ppermute | solution.py:10
  685.4 9.0 %fusion.32 = bf16[4096,1536]{0,1:T(8,128)(2,1)} fusion(f32[4096,384]{0,1:T(8,128)S(1)} %convolution_bitcast_fusion.1, f32[4096,1152]{0,1:T(8,128)S(1)} %convolution_bitcast_fusion, f32[]{:T(128)S(6)} %select_n.115), kind=kLoop, calls=%fused_computation.62 | loop fusion | flops 18874368 | bytes 37748740 | tf_op jit(solution)/shard_map/convert_element_type | solution.py:149
  694.5 139.7 %reduce-scatter.2.cloned.1.call-done = bf16[256,1536]{0,1:T(8,128)(2,1)} async-done(((bf16[4096,1536]{0,1:T(8,128)(2,1)}), bf16[256,1536]{0,1:T(8,128)(2,1)}) %reduce-scatter.2.cloned.1.call-update) | async-done | bytes 786448 | tf_op jit(solution)/shard_map/reduce_scatter | solution.py:148
  (312 shorter events, 178.8 us)
Async XLA Ops:
  13.1 6.7 copy-start.1
  13.1 8.0 copy-start.2
  13.1 138.1 %copy-start = (bf16[1,4,32,4096]{3,2,1,0:T(8,128)(2,1)S(1)}, bf16[1,4,32,4096]{3,2,1,0:T(8,128)(2,1)}, u32[]{:S(2)}) copy-start(bf16[1,4,32,4096]{3,2,1,0:T(8,128)(2,1)} %param.10) | copy-start | bytes 3145732
  13.1 136.8 %all-to-all-start = ((bf16[16,256,1152]{2,1,0:T(8,128)(2,1)}), bf16[16,256,1152]{2,1,0:T(8,128)(2,1)}, u32[]{:S(2)}, u32[]{:S(2)}) async-start(bf16[16,256,1152]{2,1,0:T(8,128)(2,1)} %stack.3), calls=%async_computation | async-start | bytes 18874368 | tf_op jit(solution)/shard_map/all_to_all | solution.py:86
  19.1 126.1 %all-gather.3.cloned.1.call-start = ((), (), s32[]{:S(2)}) async-start(), calls=%async_computation.3 | async-start | bytes 3342336 | tf_op jit(solution)/shard_map/all_gather | solution.py:88
  19.8 814.3 %reduce-scatter.2.cloned.1.call-start = ((), (), s32[]{:S(2)}) async-start(), calls=%async_computation.2 | async-start | bytes 13369344 | tf_op jit(solution)/shard_map/reduce_scatter | solution.py:148
  153.0 9.7 %collective-permute-start = (bf16[32,4096]{1,0:T(8,128)(2,1)S(1)}, bf16[32,4096]{1,0:T(8,128)(2,1)S(1)}, u32[]{:S(2)}, u32[]{:S(2)}) collective-permute-start(bf16[32,4096]{1,0:T(8,128)(2,1)S(1)} %get-tuple-element.528), channel_id=1, source_target_pairs={{16,0},{32,16},{48,32},{64,48},{80,64},{96,80},{112,96},{128,112},... | collective-permute-start | bytes 786440 | tf_op jit(solution)/shard_map/while/body/eval_jaxpr/ppermute | solution.py:10
  164.6 8.8 %collective-permute-start = (bf16[32,4096]{1,0:T(8,128)(2,1)S(1)}, bf16[32,4096]{1,0:T(8,128)(2,1)S(1)}, u32[]{:S(2)}, u32[]{:S(2)}) collective-permute-start(bf16[32,4096]{1,0:T(8,128)(2,1)S(1)} %get-tuple-element.528), channel_id=1, source_target_pairs={{16,0},{32,16},{48,32},{64,48},{80,64},{96,80},{112,96},{128,112},... | collective-permute-start | bytes 786440 | tf_op jit(solution)/shard_map/while/body/eval_jaxpr/ppermute | solution.py:10
  175.2 16.3 %collective-permute-start = (bf16[32,4096]{1,0:T(8,128)(2,1)S(1)}, bf16[32,4096]{1,0:T(8,128)(2,1)S(1)}, u32[]{:S(2)}, u32[]{:S(2)}) collective-permute-start(bf16[32,4096]{1,0:T(8,128)(2,1)S(1)} %get-tuple-element.528), channel_id=1, source_target_pairs={{16,0},{32,16},{48,32},{64,48},{80,64},{96,80},{112,96},{128,112},... | collective-permute-start | bytes 786440 | tf_op jit(solution)/shard_map/while/body/eval_jaxpr/ppermute | solution.py:10
  193.3 11.3 %collective-permute-start = (bf16[32,4096]{1,0:T(8,128)(2,1)S(1)}, bf16[32,4096]{1,0:T(8,128)(2,1)S(1)}, u32[]{:S(2)}, u32[]{:S(2)}) collective-permute-start(bf16[32,4096]{1,0:T(8,128)(2,1)S(1)} %get-tuple-element.528), channel_id=1, source_target_pairs={{16,0},{32,16},{48,32},{64,48},{80,64},{96,80},{112,96},{128,112},... | collective-permute-start | bytes 786440 | tf_op jit(solution)/shard_map/while/body/eval_jaxpr/ppermute | solution.py:10
  206.5 16.1 %collective-permute-start = (bf16[32,4096]{1,0:T(8,128)(2,1)S(1)}, bf16[32,4096]{1,0:T(8,128)(2,1)S(1)}, u32[]{:S(2)}, u32[]{:S(2)}) collective-permute-start(bf16[32,4096]{1,0:T(8,128)(2,1)S(1)} %get-tuple-element.528), channel_id=1, source_target_pairs={{16,0},{32,16},{48,32},{64,48},{80,64},{96,80},{112,96},{128,112},... | collective-permute-start | bytes 786440 | tf_op jit(solution)/shard_map/while/body/eval_jaxpr/ppermute | solution.py:10
  224.3 12.3 %collective-permute-start = (bf16[32,4096]{1,0:T(8,128)(2,1)S(1)}, bf16[32,4096]{1,0:T(8,128)(2,1)S(1)}, u32[]{:S(2)}, u32[]{:S(2)}) collective-permute-start(bf16[32,4096]{1,0:T(8,128)(2,1)S(1)} %get-tuple-element.528), channel_id=1, source_target_pairs={{16,0},{32,16},{48,32},{64,48},{80,64},{96,80},{112,96},{128,112},... | collective-permute-start | bytes 786440 | tf_op jit(solution)/shard_map/while/body/eval_jaxpr/ppermute | solution.py:10
  238.4 10.7 %collective-permute-start = (bf16[32,4096]{1,0:T(8,128)(2,1)S(1)}, bf16[32,4096]{1,0:T(8,128)(2,1)S(1)}, u32[]{:S(2)}, u32[]{:S(2)}) collective-permute-start(bf16[32,4096]{1,0:T(8,128)(2,1)S(1)} %get-tuple-element.528), channel_id=1, source_target_pairs={{16,0},{32,16},{48,32},{64,48},{80,64},{96,80},{112,96},{128,112},... | collective-permute-start | bytes 786440 | tf_op jit(solution)/shard_map/while/body/eval_jaxpr/ppermute | solution.py:10
  250.9 17.3 %collective-permute-start = (bf16[32,4096]{1,0:T(8,128)(2,1)S(1)}, bf16[32,4096]{1,0:T(8,128)(2,1)S(1)}, u32[]{:S(2)}, u32[]{:S(2)}) collective-permute-start(bf16[32,4096]{1,0:T(8,128)(2,1)S(1)} %get-tuple-element.528), channel_id=1, source_target_pairs={{16,0},{32,16},{48,32},{64,48},{80,64},{96,80},{112,96},{128,112},... | collective-permute-start | bytes 786440 | tf_op jit(solution)/shard_map/while/body/eval_jaxpr/ppermute | solution.py:10
  270.0 12.4 %collective-permute-start = (bf16[32,4096]{1,0:T(8,128)(2,1)S(1)}, bf16[32,4096]{1,0:T(8,128)(2,1)S(1)}, u32[]{:S(2)}, u32[]{:S(2)}) collective-permute-start(bf16[32,4096]{1,0:T(8,128)(2,1)S(1)} %get-tuple-element.528), channel_id=1, source_target_pairs={{16,0},{32,16},{48,32},{64,48},{80,64},{96,80},{112,96},{128,112},... | collective-permute-start | bytes 786440 | tf_op jit(solution)/shard_map/while/body/eval_jaxpr/ppermute | solution.py:10
  284.2 15.0 %collective-permute-start = (bf16[32,4096]{1,0:T(8,128)(2,1)S(1)}, bf16[32,4096]{1,0:T(8,128)(2,1)S(1)}, u32[]{:S(2)}, u32[]{:S(2)}) collective-permute-start(bf16[32,4096]{1,0:T(8,128)(2,1)S(1)} %get-tuple-element.528), channel_id=1, source_target_pairs={{16,0},{32,16},{48,32},{64,48},{80,64},{96,80},{112,96},{128,112},... | collective-permute-start | bytes 786440 | tf_op jit(solution)/shard_map/while/body/eval_jaxpr/ppermute | solution.py:10
  301.0 11.9 %collective-permute-start = (bf16[32,4096]{1,0:T(8,128)(2,1)S(1)}, bf16[32,4096]{1,0:T(8,128)(2,1)S(1)}, u32[]{:S(2)}, u32[]{:S(2)}) collective-permute-start(bf16[32,4096]{1,0:T(8,128)(2,1)S(1)} %get-tuple-element.528), channel_id=1, source_target_pairs={{16,0},{32,16},{48,32},{64,48},{80,64},{96,80},{112,96},{128,112},... | collective-permute-start | bytes 786440 | tf_op jit(solution)/shard_map/while/body/eval_jaxpr/ppermute | solution.py:10
  314.6 11.3 %collective-permute-start = (bf16[32,4096]{1,0:T(8,128)(2,1)S(1)}, bf16[32,4096]{1,0:T(8,128)(2,1)S(1)}, u32[]{:S(2)}, u32[]{:S(2)}) collective-permute-start(bf16[32,4096]{1,0:T(8,128)(2,1)S(1)} %get-tuple-element.528), channel_id=1, source_target_pairs={{16,0},{32,16},{48,32},{64,48},{80,64},{96,80},{112,96},{128,112},... | collective-permute-start | bytes 786440 | tf_op jit(solution)/shard_map/while/body/eval_jaxpr/ppermute | solution.py:10
  327.7 11.3 %collective-permute-start = (bf16[32,4096]{1,0:T(8,128)(2,1)S(1)}, bf16[32,4096]{1,0:T(8,128)(2,1)S(1)}, u32[]{:S(2)}, u32[]{:S(2)}) collective-permute-start(bf16[32,4096]{1,0:T(8,128)(2,1)S(1)} %get-tuple-element.528), channel_id=1, source_target_pairs={{16,0},{32,16},{48,32},{64,48},{80,64},{96,80},{112,96},{128,112},... | collective-permute-start | bytes 786440 | tf_op jit(solution)/shard_map/while/body/eval_jaxpr/ppermute | solution.py:10
  340.8 189.2 %collective-permute-start = (bf16[32,4096]{1,0:T(8,128)(2,1)S(1)}, bf16[32,4096]{1,0:T(8,128)(2,1)S(1)}, u32[]{:S(2)}, u32[]{:S(2)}) collective-permute-start(bf16[32,4096]{1,0:T(8,128)(2,1)S(1)} %get-tuple-element.528), channel_id=1, source_target_pairs={{16,0},{32,16},{48,32},{64,48},{80,64},{96,80},{112,96},{128,112},... | collective-permute-start | bytes 786440 | tf_op jit(solution)/shard_map/while/body/eval_jaxpr/ppermute | solution.py:10
  548.2 12.7 %collective-permute-start = (bf16[32,4096]{1,0:T(8,128)(2,1)S(1)}, bf16[32,4096]{1,0:T(8,128)(2,1)S(1)}, u32[]{:S(2)}, u32[]{:S(2)}) collective-permute-start(bf16[32,4096]{1,0:T(8,128)(2,1)S(1)} %get-tuple-element.528), channel_id=1, source_target_pairs={{16,0},{32,16},{48,32},{64,48},{80,64},{96,80},{112,96},{128,112},... | collective-permute-start | bytes 786440 | tf_op jit(solution)/shard_map/while/body/eval_jaxpr/ppermute | solution.py:10
  579.1 16.9 %collective-permute-start = (bf16[32,4096]{1,0:T(8,128)(2,1)S(1)}, bf16[32,4096]{1,0:T(8,128)(2,1)S(1)}, u32[]{:S(2)}, u32[]{:S(2)}) collective-permute-start(bf16[32,4096]{1,0:T(8,128)(2,1)S(1)} %get-tuple-element.528), channel_id=1, source_target_pairs={{16,0},{32,16},{48,32},{64,48},{80,64},{96,80},{112,96},{128,112},... | collective-permute-start | bytes 786440 | tf_op jit(solution)/shard_map/while/body/eval_jaxpr/ppermute | solution.py:10
  614.2 17.1 %collective-permute-start = (bf16[32,4096]{1,0:T(8,128)(2,1)S(1)}, bf16[32,4096]{1,0:T(8,128)(2,1)S(1)}, u32[]{:S(2)}, u32[]{:S(2)}) collective-permute-start(bf16[32,4096]{1,0:T(8,128)(2,1)S(1)} %get-tuple-element.528), channel_id=1, source_target_pairs={{16,0},{32,16},{48,32},{64,48},{80,64},{96,80},{112,96},{128,112},... | collective-permute-start | bytes 786440 | tf_op jit(solution)/shard_map/while/body/eval_jaxpr/ppermute | solution.py:10
  649.5 8.3 collective-permute-start
  659.5 22.2 %collective-permute-start = (bf16[32,4096]{1,0:T(8,128)(2,1)S(1)}, bf16[32,4096]{1,0:T(8,128)(2,1)S(1)}, u32[]{:S(2)}, u32[]{:S(2)}) collective-permute-start(bf16[32,4096]{1,0:T(8,128)(2,1)S(1)} %get-tuple-element.528), channel_id=1, source_target_pairs={{16,0},{32,16},{48,32},{64,48},{80,64},{96,80},{112,96},{128,112},... | collective-permute-start | bytes 786440 | tf_op jit(solution)/shard_map/while/body/eval_jaxpr/ppermute | solution.py:10
Sparse Core Ops, SparseCore 0:
  21.8 123.3 all-gather.2
  694.6 139.5 reduce-scatter.1
